TPU v7x, 32 devices: a whole 2x2x4 slice. The times are simulated.
32 devices in a mesh: pole: 4 (over y, core), snode: 8 (over z, x).
Axes of the slice: x: 2, y: 2, z: 4, core: 2. Of those that a mesh axis runs over, the one named last changes fastest.
Arguments:
- pivot_inverse: float32 [8, 16, 2, 256, 256], P('pole', 'snode'), as said below
- factor_block: float32 [8, 16, 2, 256, 256], P('pole', 'snode')
- live_width_array: int32 [16], P('snode'), may hold values from 128 to 256, as said below
- pole_weight: float32 [8, 2], P('pole'), may hold values from -4 to 4
Outputs:
- density_diag: float32 [16, 256, 256], P('snode')
- density_off: float32 [16, 256, 256], P('snode')
Inputs may be any that keep to these rules, and one draw needn't show every extreme that they name: `live_width_array`: live widths of the supernodes; at least one supernode is 256 wide and one is 128 wide. `pivot_inverse`: symmetric in its last two dimensions with a dominant real diagonal.
All inputs are finite; a program needn't handle non-finite values.
Results may differ from a plain program's by a relative error of at most 0.0003.
Values sent between devices are 32-bit elements; how exact they have to be, the bound alone decides.
No kernel may reach another device: no remote copies, remote signals or barrier semaphores. Data moves between devices by JAX's collectives and lax.ppermute only.
A program may use at most 192 MiB of HBM per device.

v0:
```python
import jax
import jax.numpy as jnp
from jax import lax
from jax.sharding import PartitionSpec as P


def passed_along(value, axis, steps):
    count = lax.axis_size(axis)
    first, last = (max(0, -steps), min(count, count - steps))
    return lax.ppermute(value, axis, [(source, source + steps) for source in range(first, last)])


def multiply_real(left, right):
    return jnp.einsum("...ij,...jk->...ik", left, right, precision=lax.Precision.HIGHEST)


def complex_product(left, right):
    left_real = left[..., 0, :, :]
    leading_imaginary = left[..., 1, :, :]
    right_re = right[..., 0, :, :]
    right_im = right[..., 1, :, :]
    real_part = multiply_real(left_real, right_re) - multiply_real(leading_imaginary, right_im)
    imag_part = multiply_real(left_real, right_im) + multiply_real(leading_imaginary, right_re)
    return jnp.stack([real_part, imag_part], axis=-3)


def transpose_block(block):
    return jnp.swapaxes(block, -1, -2)


def local(pivot_inverse, factor_block, live_width_array, pole_weight):
    width = pivot_inverse.shape[-1]
    local_count = pivot_inverse.shape[1]
    columns = jnp.arange(width, dtype=jnp.int32)
    keep = (columns[None, :] < live_width_array[:, None]).astype(jnp.float32)
    pivot = pivot_inverse * keep[None, :, None, :, None] * keep[None, :, None, None, :]
    factor = factor_block * keep[None, :, None, None, :]

    def sweep_local(parent):
        reciprocal_matrices = []
        offsets = []
        for slot in range(local_count):
            link = factor[:, slot]
            product = complex_product(parent, link)
            parent = pivot[:, slot] + complex_product(transpose_block(link), product)
            reciprocal_matrices.append(parent)
            offsets.append(-product)
        return (jnp.stack(reciprocal_matrices, axis=1), jnp.stack(offsets, axis=1))

    position = lax.axis_index("snode")
    turns = lax.axis_size("snode")

    def one_turn(count, carry):
        reciprocal_matrices, offsets = carry
        incoming = passed_along(reciprocal_matrices[:, -1], "snode", 1)
        return lax.cond(
            position == count, sweep_local, lambda value: (reciprocal_matrices, offsets), incoming
        )

    empty = jnp.zeros(pivot.shape, jnp.float32)
    reciprocal_matrices, offsets = lax.fori_loop(0, turns, one_turn, (empty, empty))
    weight_re = pole_weight[:, 0][:, None, None, None]
    weight_im = pole_weight[:, 1][:, None, None, None]
    diag_local = jnp.sum(
        weight_re * reciprocal_matrices[:, :, 1] + weight_im * reciprocal_matrices[:, :, 0], axis=0
    )
    off_local = jnp.sum(weight_re * offsets[:, :, 1] + weight_im * offsets[:, :, 0], axis=0)
    density_diag, density_off = lax.psum((diag_local, off_local), "pole")
    return (density_diag, density_off)


def solution(mesh):
    placed = (
        P("pole", "snode", None, None, None),
        P("pole", "snode", None, None, None),
        P("snode"),
        P("pole", None),
    )
    return jax.shard_map(
        local,
        mesh=mesh,
        in_specs=placed,
        out_specs=(P("snode", None, None), P("snode", None, None)),
        check_vma=False,
    )
```

profile of v0, /device:TPU:29, one launch (start us, length us, event | category | flops | bytes accessed | tf_op | source)
XLA Modules:
  0.0 472.9 jit_solution(2081354883348924695)
XLA Ops:
  7.9 4.4 copy_multiply_fusion
  12.4 1.9 copy.30
  14.5 1.5 broadcast_in_dim.2
  16.0 1.5 broadcast_in_dim.2.clone
  17.5 377.2 %while.15 = (s32[]{:T(128)}, f32[2,2,2,256,256]{3,4,0,2,1:T(8,128)}, f32[2,2,2,256,256]{4,3,0,2,1:T(8,128)}, s32[]{:T(128)}, f32[2,2,2,256,256]{3,4,0,2,1:T(8,12...) while((s32[]{:T(128)}, f32[2,2,2,256,256]{3,4,0,2,1:T(8,128)}, f32[2,2,2,256,256]{4,3,0,2,1:T(8,128)}, ...), condition=%wide.region_3.0_spmd, body=%wide.region_0.0_spmd.sunk | while | flops 6447169536 | bytes 68157640 | solution.py:61
  17.5 2.9 copy.63
  20.4 2.4 slice_bitcast_fusion.39
  22.8 3.1 collective-permute-start
  25.9 23.9 %collective-permute-done = f32[2,2,256,256]{3,2,0,1:T(8,128)S(1)} collective-permute-done((f32[2,2,256,256]{3,2,0,1:T(8,128)}, f32[2,2,256,256]{3,2,0,1:T(8,128)S(1)}, u32[]{:S(2)}, u32[]{:S(2)}) %collective-permute-start) | collective-permute-done | bytes 1048608 | tf_op jit(solution)/shard_map/while/body/eval_jaxpr/ppermute | solution.py:10
  49.8 2.9 copy.63
  52.7 2.4 slice_bitcast_fusion.39
  55.1 2.2 collective-permute-start
  57.3 23.9 %collective-permute-done = f32[2,2,256,256]{3,2,0,1:T(8,128)S(1)} collective-permute-done((f32[2,2,256,256]{3,2,0,1:T(8,128)}, f32[2,2,256,256]{3,2,0,1:T(8,128)S(1)}, u32[]{:S(2)}, u32[]{:S(2)}) %collective-permute-start) | collective-permute-done | bytes 1048608 | tf_op jit(solution)/shard_map/while/body/eval_jaxpr/ppermute | solution.py:10
  81.1 2.9 copy.63
  84.1 2.4 slice_bitcast_fusion.39
  86.4 1.9 collective-permute-start
  88.3 23.3 %collective-permute-done = f32[2,2,256,256]{3,2,0,1:T(8,128)S(1)} collective-permute-done((f32[2,2,256,256]{3,2,0,1:T(8,128)}, f32[2,2,256,256]{3,2,0,1:T(8,128)S(1)}, u32[]{:S(2)}, u32[]{:S(2)}) %collective-permute-start) | collective-permute-done | bytes 1048608 | tf_op jit(solution)/shard_map/while/body/eval_jaxpr/ppermute | solution.py:10
  111.6 2.9 copy.63
  114.5 2.4 slice_bitcast_fusion.39
  116.9 1.9 collective-permute-start
  118.8 22.3 %collective-permute-done = f32[2,2,256,256]{3,2,0,1:T(8,128)S(1)} collective-permute-done((f32[2,2,256,256]{3,2,0,1:T(8,128)}, f32[2,2,256,256]{3,2,0,1:T(8,128)S(1)}, u32[]{:S(2)}, u32[]{:S(2)}) %collective-permute-start) | collective-permute-done | bytes 1048608 | tf_op jit(solution)/shard_map/while/body/eval_jaxpr/ppermute | solution.py:10
  141.1 2.9 copy.63
  144.0 2.4 slice_bitcast_fusion.39
  146.4 1.9 collective-permute-start
  148.3 21.4 %collective-permute-done = f32[2,2,256,256]{3,2,0,1:T(8,128)S(1)} collective-permute-done((f32[2,2,256,256]{3,2,0,1:T(8,128)}, f32[2,2,256,256]{3,2,0,1:T(8,128)S(1)}, u32[]{:S(2)}, u32[]{:S(2)}) %collective-permute-start) | collective-permute-done | bytes 1048608 | tf_op jit(solution)/shard_map/while/body/eval_jaxpr/ppermute | solution.py:10
  169.7 2.9 copy.63
  172.7 2.4 slice_bitcast_fusion.39
  175.0 1.9 collective-permute-start
  176.9 20.5 %collective-permute-done = f32[2,2,256,256]{3,2,0,1:T(8,128)S(1)} collective-permute-done((f32[2,2,256,256]{3,2,0,1:T(8,128)}, f32[2,2,256,256]{3,2,0,1:T(8,128)S(1)}, u32[]{:S(2)}, u32[]{:S(2)}) %collective-permute-start) | collective-permute-done | bytes 1048608 | tf_op jit(solution)/shard_map/while/body/eval_jaxpr/ppermute | solution.py:10
  197.4 2.9 copy.63
  200.3 2.4 slice_bitcast_fusion.39
  202.7 1.9 collective-permute-start
  204.6 141.2 %collective-permute-done = f32[2,2,256,256]{3,2,0,1:T(8,128)S(1)} collective-permute-done((f32[2,2,256,256]{3,2,0,1:T(8,128)}, f32[2,2,256,256]{3,2,0,1:T(8,128)S(1)}, u32[]{:S(2)}, u32[]{:S(2)}) %collective-permute-start) | collective-permute-done | bytes 1048608 | tf_op jit(solution)/shard_map/while/body/eval_jaxpr/ppermute | solution.py:10
  345.8 21.4 %conditional.2 = ((f32[2,2,2,256,256]{3,4,0,2,1:T(8,128)}, f32[2,2,2,256,256]{4,3,0,2,1:T(8,128)})) conditional(s32[]{:T(128)} %convert_element_type.21, (f32[2,2,2,256,256]{3,4,0,2,1:T(8,128)}, f32[2,2,2,256,256]{4,3,0,2,1:T(8,128)}) %tuple.50, (f32[2,2,2,256,256]{3,4,0,2,1:T(8,128)S(1)}, f32[2,2,256,256]{3,2,0,1:T(8,128)S(1)}, ...), branch_computations={%region_1.0_spmd, %region_2.0_spmd} | conditional | flops 6447169536 | bytes 57671704 | solution.py:56
  345.8 2.0 slice_bitcast_fusion
  360.3 1.1 fusion
  362.4 1.1 fusion.1
  363.9 1.5 pad_maximum_fusion
  365.6 1.6 pad_maximum_fusion.1
  367.2 2.9 copy.63
  370.1 2.4 slice_bitcast_fusion.39
  372.4 1.9 collective-permute-start
  374.4 20.3 %collective-permute-done = f32[2,2,256,256]{3,2,0,1:T(8,128)S(1)} collective-permute-done((f32[2,2,256,256]{3,2,0,1:T(8,128)}, f32[2,2,256,256]{3,2,0,1:T(8,128)S(1)}, u32[]{:S(2)}, u32[]{:S(2)}) %collective-permute-start) | collective-permute-done | bytes 1048608 | tf_op jit(solution)/shard_map/while/body/eval_jaxpr/ppermute | solution.py:10
  394.7 3.1 copy.31
  397.8 3.0 fusion.21
  400.8 61.5 %all-reduce.3.cloned.1.call-done = (f32[2,256,256]{2,1,0:T(8,128)}, f32[2,256,256]{2,1,0:T(8,128)}) async-done(((f32[2,256,256]{2,1,0:T(8,128)}, f32[2,256,256]{2,1,0:T(8,128)}), (f32[2,256,256]{2,1,0:T(8,128)}, f32[2,256,256]{2,1,0:T(8,128)})) %all-reduce.3.cloned.1.call-update) | async-done | bytes 1048592 | tf_op jit(solution)/shard_map/psum | solution.py:68
  462.3 1.9 copy.81
  464.2 1.9 copy.82
  (32 shorter events, 15.0 us)
Async XLA Ops:
  7.2 455.2 %all-reduce.3.cloned.1.call-start = ((), (), s32[]{:S(2)}) async-start(), calls=%async_computation | async-start | bytes 2097152 | tf_op jit(solution)/shard_map/psum | solution.py:68
  12.4 1.9 copy-start.1
  22.8 27.0 %collective-permute-start = (f32[2,2,256,256]{3,2,0,1:T(8,128)}, f32[2,2,256,256]{3,2,0,1:T(8,128)S(1)}, u32[]{:S(2)}, u32[]{:S(2)}) collective-permute-start(f32[2,2,256,256]{3,2,0,1:T(8,128)} %slice_bitcast_fusion.39), channel_id=1, source_target_pairs={{0,1},{1,2},{2,3},{3,4},{4,5},{5,6},{6,7},{8,9},{9,10},{10,11},{11... | collective-permute-start | bytes 3145736 | tf_op jit(solution)/shard_map/while/body/eval_jaxpr/ppermute | solution.py:10
  55.1 26.1 %collective-permute-start = (f32[2,2,256,256]{3,2,0,1:T(8,128)}, f32[2,2,256,256]{3,2,0,1:T(8,128)S(1)}, u32[]{:S(2)}, u32[]{:S(2)}) collective-permute-start(f32[2,2,256,256]{3,2,0,1:T(8,128)} %slice_bitcast_fusion.39), channel_id=1, source_target_pairs={{0,1},{1,2},{2,3},{3,4},{4,5},{5,6},{6,7},{8,9},{9,10},{10,11},{11... | collective-permute-start | bytes 3145736 | tf_op jit(solution)/shard_map/while/body/eval_jaxpr/ppermute | solution.py:10
  86.4 25.2 %collective-permute-start = (f32[2,2,256,256]{3,2,0,1:T(8,128)}, f32[2,2,256,256]{3,2,0,1:T(8,128)S(1)}, u32[]{:S(2)}, u32[]{:S(2)}) collective-permute-start(f32[2,2,256,256]{3,2,0,1:T(8,128)} %slice_bitcast_fusion.39), channel_id=1, source_target_pairs={{0,1},{1,2},{2,3},{3,4},{4,5},{5,6},{6,7},{8,9},{9,10},{10,11},{11... | collective-permute-start | bytes 3145736 | tf_op jit(solution)/shard_map/while/body/eval_jaxpr/ppermute | solution.py:10
  116.9 24.3 %collective-permute-start = (f32[2,2,256,256]{3,2,0,1:T(8,128)}, f32[2,2,256,256]{3,2,0,1:T(8,128)S(1)}, u32[]{:S(2)}, u32[]{:S(2)}) collective-permute-start(f32[2,2,256,256]{3,2,0,1:T(8,128)} %slice_bitcast_fusion.39), channel_id=1, source_target_pairs={{0,1},{1,2},{2,3},{3,4},{4,5},{5,6},{6,7},{8,9},{9,10},{10,11},{11... | collective-permute-start | bytes 3145736 | tf_op jit(solution)/shard_map/while/body/eval_jaxpr/ppermute | solution.py:10
  146.4 23.3 %collective-permute-start = (f32[2,2,256,256]{3,2,0,1:T(8,128)}, f32[2,2,256,256]{3,2,0,1:T(8,128)S(1)}, u32[]{:S(2)}, u32[]{:S(2)}) collective-permute-start(f32[2,2,256,256]{3,2,0,1:T(8,128)} %slice_bitcast_fusion.39), channel_id=1, source_target_pairs={{0,1},{1,2},{2,3},{3,4},{4,5},{5,6},{6,7},{8,9},{9,10},{10,11},{11... | collective-permute-start | bytes 3145736 | tf_op jit(solution)/shard_map/while/body/eval_jaxpr/ppermute | solution.py:10
  175.0 22.4 %collective-permute-start = (f32[2,2,256,256]{3,2,0,1:T(8,128)}, f32[2,2,256,256]{3,2,0,1:T(8,128)S(1)}, u32[]{:S(2)}, u32[]{:S(2)}) collective-permute-start(f32[2,2,256,256]{3,2,0,1:T(8,128)} %slice_bitcast_fusion.39), channel_id=1, source_target_pairs={{0,1},{1,2},{2,3},{3,4},{4,5},{5,6},{6,7},{8,9},{9,10},{10,11},{11... | collective-permute-start | bytes 3145736 | tf_op jit(solution)/shard_map/while/body/eval_jaxpr/ppermute | solution.py:10
  202.7 143.1 %collective-permute-start = (f32[2,2,256,256]{3,2,0,1:T(8,128)}, f32[2,2,256,256]{3,2,0,1:T(8,128)S(1)}, u32[]{:S(2)}, u32[]{:S(2)}) collective-permute-start(f32[2,2,256,256]{3,2,0,1:T(8,128)} %slice_bitcast_fusion.39), channel_id=1, source_target_pairs={{0,1},{1,2},{2,3},{3,4},{4,5},{5,6},{6,7},{8,9},{9,10},{10,11},{11... | collective-permute-start | bytes 3145736 | tf_op jit(solution)/shard_map/while/body/eval_jaxpr/ppermute | solution.py:10
  372.4 22.2 %collective-permute-start = (f32[2,2,256,256]{3,2,0,1:T(8,128)}, f32[2,2,256,256]{3,2,0,1:T(8,128)S(1)}, u32[]{:S(2)}, u32[]{:S(2)}) collective-permute-start(f32[2,2,256,256]{3,2,0,1:T(8,128)} %slice_bitcast_fusion.39), channel_id=1, source_target_pairs={{0,1},{1,2},{2,3},{3,4},{4,5},{5,6},{6,7},{8,9},{9,10},{10,11},{11... | collective-permute-start | bytes 3145736 | tf_op jit(solution)/shard_map/while/body/eval_jaxpr/ppermute | solution.py:10
  394.7 3.1 copy-start
Sparse Core Ops, SparseCore 0:
  400.9 61.3 all-reduce.2
where the time goes:
time: 476 us; the launch traced here: 473 us
  waiting for transfers between devices  358 us (75%)
  local copies, waits for them, and re-layouts  56.1 us (12%)
  starting transfers between devices  16.8 us (4%)
  matrix products  15.4 us (3%)
  between operations  14.1 us (3%)
  other arithmetic  12 us (3%)
    ppermute x8, waiting for transfers between devices, passed_along(): lax.ppermute(value, axis, [(source, source + steps) for source in range(f...  297 us
    psum x1, waiting for transfers between devices, local(): density_diag, density_off = lax.psum((diag_local, off_local), 'pole')  61.5 us
    another operation x8, local copies, waits for them, and re-layouts  23.3 us
    squeeze x8, local copies, waits for them, and re-layouts, one_turn(): incoming = passed_along(reciprocal_matrices[:, -1], 'snode', 1)  18.9 us
    ppermute x8, starting transfers between devices, passed_along(): lax.ppermute(value, axis, [(source, source + steps) for source in range(f...  16.8 us
    dot_general x16, matrix products, multiply_real(): jnp.einsum('...ij,...jk->...ik', left, right, precision=lax.Precision.HIG...  15.4 us
  transfers between devices with their start and end apart: 9, of which 9 were waited for; matrix products, arithmetic and copies ran while one was open for 0% of the time, Pallas kernels for 0%

commit v1 on v0

v1 whole, which is shorter than its diff:
```python
import functools

import jax
import jax.numpy as jnp
from jax import lax
from jax.experimental import pallas as pl
from jax.experimental.pallas import tpu as pltpu
from jax.sharding import PartitionSpec as P

F32 = jnp.float32
BF16 = jnp.bfloat16
AXES = ("pole", "snode")
VMEM_LIMIT = 40 * 1024 * 1024


def halves(value):
    high = value.astype(BF16)
    return high, (value - high.astype(F32)).astype(BF16)


def split_pair(real, imag):
    (rh, rl), (ih, il) = halves(real), halves(imag)
    return rh, ih, rl, il


def dot(left, right):
    return jnp.dot(left, right, preferred_element_type=F32)


def dot3(lh, ll, rh, rl):
    return dot(lh, rh) + (dot(lh, rl) + dot(ll, rh))


def complex_dot(left, right):
    arh, aih, arl, ail = left
    brh, bih, brl, bil = right
    real = dot3(arh, arl, brh, brl) - dot3(aih, ail, bih, bil)
    imag = dot3(arh, arl, bih, bil) + dot3(aih, ail, brh, brl)
    return real, imag


def rows_columns(size):
    return (
        lax.broadcasted_iota(jnp.int32, (size, size), 0),
        lax.broadcasted_iota(jnp.int32, (size, size), 1),
    )


def packed(block):
    half = block.shape[0] // 2
    row, column = rows_columns(half)
    lower = block[half:, half:]
    mixed = jnp.where(row >= column, block[:half, :half], lower)
    diagonal = jnp.sum(jnp.where(row == column, lower, 0.0), axis=0, keepdims=True)
    return jnp.concatenate(
        [block[:half, half:], mixed, jnp.broadcast_to(diagonal, (8, half))], axis=0
    )


def unpacked(value):
    half = value.shape[1]
    row, column = rows_columns(half)
    right, mixed = value[:half], value[half : 2 * half]
    diagonal = value[2 * half : 2 * half + 1]
    turned = mixed.T
    first = jnp.where(row >= column, mixed, turned)
    last = jnp.where(row < column, mixed, jnp.where(row == column, diagonal, turned))
    return jnp.concatenate(
        [jnp.concatenate([first, right], axis=1), jnp.concatenate([right.T, last], axis=1)], axis=0
    )


def unpacked_split(ref):
    return split_pair(unpacked(ref[0]), unpacked(ref[1]))


def load4(ref):
    return tuple(ref[i] for i in range(4))


def store4(ref, parts):
    for i, part in enumerate(parts):
        ref[i] = part


def prepare_kernel(slot, live, weight, pivot, factor, f0s, f0t, gs, gt, g, e, weighted):
    width = pivot.shape[-1]
    row, column = rows_columns(width)
    d, f = [], []
    for k in range(2):
        columns = column < live[k]
        both = jnp.logical_and(row < live[k], columns)
        d.append([jnp.where(both, pivot[0, k, c], 0.0) for c in range(2)])
        f.append([jnp.where(columns, factor[0, k, c], 0.0) for c in range(2)])
    s0, s1 = split_pair(*f[0]), split_pair(*f[1])
    store4(f0s, s0)
    store4(f0t, split_pair(f[0][0].T, f[0][1].T))
    gr, gi = complex_dot(s0, s1)
    g[0], g[1] = gr, gi
    store4(gs, split_pair(gr, gi))
    store4(gt, split_pair(gr.T, gi.T))
    br, bi = complex_dot(split_pair(*d[0]), s1)
    tr, ti = complex_dot(split_pair(f[1][0].T, f[1][1].T), split_pair(br, bi))
    er, ei = d[1][0] + tr, d[1][1] + ti
    e[0], e[1] = packed(er), packed(ei)
    w0, w1 = weight[slot[0], 0], weight[slot[0], 1]
    weighted[0] = packed(w1 * d[0][0] + w0 * d[0][1])
    weighted[1] = packed(w1 * er + w0 * ei)
    b = w1 * br + w0 * bi
    half = width // 2
    weighted_b = jnp.concatenate([b[:, :half], b[:, half:]], axis=0)
    weighted[2] = weighted_b[: width + 8]
    weighted[3, : width - 8] = weighted_b[width + 8 :]


def fold(x, gs, gt, e, out):
    tr, ti = complex_dot(x, load4(gs))
    yr, yi = complex_dot(load4(gt), split_pair(tr, ti))
    out[0] = e[0] + packed(yr)
    out[1] = e[1] + packed(yi)


def step_kernel(active, gs, gt, e, *refs):
    *received, out = refs

    @pl.when(active[0] == 1)
    def _():
        value = received[0][...]
        for other in received[1:]:
            value = value + other[...]
        fold(split_pair(unpacked(value[0]), unpacked(value[1])), gs, gt, e, out)


def pair_kernel(odd, g, e, g_in, e_in, fas, fat, ea, ps, pt, ep):
    is_odd = odd[0] == 1
    ga = [jnp.where(is_odd, g_in[c], g[c]) for c in range(2)]
    gb = [jnp.where(is_odd, g[c], g_in[c]) for c in range(2)]
    low = [jnp.where(is_odd, e_in[c], e[c]) for c in range(2)]
    high = [jnp.where(is_odd, e[c], e_in[c]) for c in range(2)]
    sa, sb = split_pair(*ga), split_pair(*gb)
    store4(fas, sa)
    store4(fat, split_pair(ga[0].T, ga[1].T))
    pr, pi = complex_dot(sa, sb)
    store4(ps, split_pair(pr, pi))
    store4(pt, split_pair(pr.T, pi.T))
    br, bi = complex_dot(split_pair(unpacked(low[0]), unpacked(low[1])), sb)
    tr, ti = complex_dot(split_pair(gb[0].T, gb[1].T), split_pair(br, bi))
    for c, term in enumerate((tr, ti)):
        ea[c] = low[c]
        ep[c] = high[c] + packed(term)


def share_kernel(odd, fas, fat, ea, *refs):
    *received, own, sent, scratch = refs
    value = received[0][...]
    for other in received[1:]:
        value = value + other[...]
    fold(split_pair(unpacked(value[0]), unpacked(value[1])), fas, fat, ea, scratch)
    is_odd = odd[0] == 1
    own[...] = jnp.where(is_odd, scratch[...], value)
    sent[...] = jnp.where(is_odd, value, scratch[...])


def density_kernel(slot, core, weight, x, f0s, f0t, gs, gt, weighted, *refs):
    *before, out = refs
    width = f0s.shape[-1]
    half = width // 2
    tall = width + 8
    w0, w1 = weight[slot[0], 0], weight[slot[0], 1]
    xs = unpacked_split(x)
    pr, pi = complex_dot(xs, load4(f0s))
    qr, qi = complex_dot(xs, load4(gs))
    u, v = w1 * pr + w0 * pi, w0 * pr - w1 * pi
    s, t = w1 * qr + w0 * qi, w0 * qr - w1 * qi
    us, ts = split_pair(u, v), split_pair(s, t)
    f, g = load4(f0t), load4(gt)

    def real_of(left, right):
        return dot3(left[0], left[2], right[0], right[2]) + dot3(left[1], left[3], right[1], right[3])

    def flat(block):
        return jnp.concatenate([block[:, :half], block[:, half:]], axis=0)

    second = flat(real_of(f, ts))
    first_entry, second_entry = core[0], 1 - core[0]

    def put(entry, start, stop, value):
        if before:
            value = value + before[0][entry, start:stop]
        out[entry, start:stop] = value

    put(first_entry, 0, 2 * width, flat(-u))
    put(first_entry, 2 * width, 2 * width + tall, weighted[0] + packed(real_of(f, us)))
    put(second_entry, 0, tall, -(second[:tall] + weighted[2]))
    put(second_entry, tall, 2 * width, -(second[tall:] + weighted[3, : width - 8]))
    put(second_entry, 2 * width, 2 * width + tall, weighted[1] + packed(real_of(g, ts)))


def unpack_kernel(core, mine, theirs, diag, off):
    width = diag.shape[-1]
    half = width // 2
    for source, entry in ((mine, core[0]), (theirs, 1 - core[0])):
        off[entry, :, :half] = source[:width]
        off[entry, :, half:] = source[width : 2 * width]
        diag[entry] = unpacked(source[2 * width :])


SCALAR = pl.BlockSpec(memory_space=pltpu.SMEM)
WHOLE = pl.BlockSpec(memory_space=pltpu.VMEM)


def run(kernel, scalars, arrays, shapes, dots, scratch=()):
    size = sum(a.size * a.dtype.itemsize for a in arrays)
    return pl.pallas_call(
        kernel,
        out_shape=shapes,
        in_specs=[SCALAR] * len(scalars) + [WHOLE] * len(arrays),
        out_specs=[WHOLE] * len(shapes),
        scratch_shapes=list(scratch),
        compiler_params=pltpu.CompilerParams(vmem_limit_bytes=VMEM_LIMIT),
        cost_estimate=pl.CostEstimate(flops=2 * dots * 256**3, bytes_accessed=size, transcendentals=0),
    )(*scalars, *arrays)


def one(value):
    return jnp.asarray(value, jnp.int32).reshape(1)


def prepare(slot, live, weight, pivot, factor):
    width = pivot.shape[-1]
    quarter = (width + 8, width // 2)
    block = (1,) + pivot.shape[1:]
    parts = jax.ShapeDtypeStruct((4, width, width), BF16)
    shapes = [parts] * 4 + [
        jax.ShapeDtypeStruct((2, width, width), F32),
        jax.ShapeDtypeStruct((2,) + quarter, F32),
        jax.ShapeDtypeStruct((4,) + quarter, F32),
    ]
    chosen = pl.BlockSpec(block, lambda i, s, l: (s[0], 0, 0, 0, 0))
    return pl.pallas_call(
        lambda slot, live, weight, pivot, factor, *outs: prepare_kernel(
            slot, live, weight, pivot, factor, *outs
        ),
        out_shape=shapes,
        grid_spec=pltpu.PrefetchScalarGridSpec(
            num_scalar_prefetch=2,
            grid=(1,),
            in_specs=[SCALAR, chosen, chosen],
            out_specs=[pl.BlockSpec(s.shape, lambda i, s_, l, n=len(s.shape): (0,) * n) for s in shapes],
        ),
        compiler_params=pltpu.CompilerParams(vmem_limit_bytes=VMEM_LIMIT),
        cost_estimate=pl.CostEstimate(flops=2 * 36 * width**3, bytes_accessed=6 * 2**20, transcendentals=0),
    )(slot, live, weight, pivot, factor)


def local(pivot, factor, live, weight):
    poles, turns = lax.axis_size("pole"), lax.axis_size("snode")
    rows = turns // 2
    pole, place = lax.axis_index("pole"), lax.axis_index("snode")
    row, odd, core = place // 2, place % 2, pole % 2
    width = pivot.shape[-1]
    quarter = (width + 8, width // 2)
    mirrored = jax.ShapeDtypeStruct((2,) + quarter, F32)
    parts = jax.ShapeDtypeStruct((4, width, width), BF16)

    def at(pole_index, snode_index):
        return pole_index * turns + snode_index

    def host(row_index, pole_index, wave):
        if row_index == 0:
            return 1
        return 2 * row_index + 1 - (pole_index % 2 ^ wave)

    hosted = jnp.where(row == 0, 1 - odd, jnp.where(odd == 1 - core, 0, 1))
    mine, other = one(hosted), one(1 - hosted)
    odd_flag, core_flag = one(odd), one(core)

    swaps = [
        (at(p, s), at(p, s ^ 1)) for p in range(poles) for s in range(2, turns)
    ]
    first = [(at(p, 0), at(p, 1)) for p in range(poles)]

    o_f0s, o_f0t, o_gs, o_gt, o_g, o_e, o_w = prepare(other, live, weight, pivot, factor)
    e_in = lax.ppermute(o_e, AXES, first + swaps)
    m_f0s, m_f0t, m_gs, m_gt, m_g, m_e, m_w = prepare(mine, live, weight, pivot, factor)
    g_in = lax.ppermute(o_g, AXES, swaps)
    e_second = lax.ppermute(m_e, AXES, first)

    starts = one(place == 1)
    (wave_a,) = run(step_kernel, [starts], [m_gs, m_gt, m_e, e_in], [mirrored], 24)
    (wave_b,) = run(step_kernel, [starts], [o_gs, o_gt, o_e, e_second], [mirrored], 24)

    received = []
    if rows > 1:
        received.append(
            lax.ppermute(wave_a, AXES, [(at(p, 1), at(p, host(1, p, 0))) for p in range(poles)])
        )
        received.append(
            lax.ppermute(wave_b, AXES, [(at(p, 1), at(p, host(1, p, 1))) for p in range(poles)])
        )
    fas, fat, ea, ps, pt, ep = run(
        pair_kernel,
        [odd_flag],
        [m_g, m_e, g_in, e_in],
        [parts, parts, mirrored, parts, parts, mirrored],
        36,
    )
    arrived = list(received)
    for turn in range(1, rows - 1):
        (wave,) = run(step_kernel, [one(row == turn)], [ps, pt, ep] + arrived, [mirrored], 24)
        arrived = [
            lax.ppermute(
                wave,
                AXES,
                [
                    (at(p, host(turn, p, w)), at(p, host(turn + 1, p, w)))
                    for p in range(poles)
                    for w in range(2)
                ],
            )
        ]
        received += arrived
    if not received:
        received = [jnp.zeros(mirrored.shape, F32)]
    own, sent = run(
        share_kernel,
        [odd_flag],
        [fas, fat, ea] + received,
        [mirrored, mirrored],
        24,
        [pltpu.VMEM(mirrored.shape, F32)],
    )
    both = [(at(p, s), at(p, s ^ 1)) for p in range(poles) for s in range(turns)]
    shared = lax.ppermute(sent, AXES, both)

    total = jax.ShapeDtypeStruct((2, 3 * width + 8, width // 2), F32)
    (sums,) = run(
        density_kernel, [mine, core_flag, weight], [own, m_f0s, m_f0t, m_gs, m_gt, m_w], [total], 42
    )
    (sums,) = run(
        density_kernel,
        [other, core_flag, weight],
        [shared, o_f0s, o_f0t, o_gs, o_gt, o_w, sums],
        [total],
        42,
    )
    def exchanged(value, distance):
        return lax.ppermute(value, "pole", [(p, p ^ distance) for p in range(poles)])

    kept = sums[0] + exchanged(sums[1], 1)
    distance = 2
    while distance < poles:
        kept = kept + exchanged(kept, distance)
        distance *= 2
    theirs = exchanged(kept, 1)
    full = jax.ShapeDtypeStruct((2, width, width), F32)
    return tuple(run(unpack_kernel, [core_flag], [kept, theirs], [full, full], 0))


def solution(mesh):
    placed = (
        P("pole", "snode", None, None, None),
        P("pole", "snode", None, None, None),
        P("snode"),
        P("pole", None),
    )
    return jax.shard_map(
        local,
        mesh=mesh,
        in_specs=placed,
        out_specs=(P("snode", None, None), P("snode", None, None)),
        check_vma=False,
    )
```

time: 476 us -> 98.1 us (0.21)
  waiting for transfers between devices: 358 us -> 32.5 us
  local copies, waits for them, and re-layouts: 56.1 us -> 25.1 us
  matrix products: 15.4 us -> 0 us
  Pallas kernels: 0 us -> 15.1 us
  between operations: 14.1 us -> 0.99 us
  other arithmetic: 12 us -> 0.11 us
  starting transfers between devices: 16.8 us -> 23.6 us
    ppermute x8 -> x11, waiting for transfers between devices: 297 us -> 32.5 us  [the longest x3 12.9 us: exchanged(): lax.ppermute(value, 'pole', [(p, p ^ distance) for p in range(poles)])]
    psum x1 -> x0, waiting for transfers between devices: 61.5 us -> none  [local(): density_diag, density_off = lax.psum((diag_local, off_local), 'pole')]
    another operation x8 -> x0, local copies, waits for them, and re-layouts: 23.3 us -> none
    unnamed x6 -> x82, local copies, waits for them, and re-layouts: 3.74 us -> 25.1 us
    squeeze x8 -> x1, local copies, waits for them, and re-layouts: 18.9 us -> 0.03 us  [local(): kept = sums[0] + exchanged(sums[1], 1)]
    dot_general x16 -> x0, matrix products: 15.4 us -> none  [multiply_real(): jnp.einsum('...ij,...jk->...ik', left, right, precision=lax.Precision.HIG...]
    pallas_call x0 -> x11, Pallas kernels: none -> 15.1 us  [the longest x9 9.4 us: run(): pl.pallas_call(kernel, out_shape=shapes, in_specs=[SCALAR] * len(scalars)...]
    ppermute x8 -> x11, starting transfers between devices: 16.8 us -> 23.6 us  [the longest x1 7.91 us: local(): shared = lax.ppermute(sent, AXES, both)]
  transfers between devices with their start and end apart: 9 -> 11, of which waited for: 9 -> 6; matrix products, arithmetic and copies ran while one was open for 0% -> 0% of each run, Pallas kernels for 0% -> 7%
where the time goes in v1:
time: 98.1 us; the launch traced here: 97.4 us
  waiting for transfers between devices  32.5 us (33%)
  local copies, waits for them, and re-layouts  25.1 us (26%)
  starting transfers between devices  23.6 us (24%)
  Pallas kernels  15.1 us (15%)
  between operations  0.99 us (1%)
    unnamed x82, local copies, waits for them, and re-layouts  25.1 us
    ppermute x3, waiting for transfers between devices, exchanged(): lax.ppermute(value, 'pole', [(p, p ^ distance) for p in range(poles)])  12.9 us
    ppermute x2, waiting for transfers between devices, local(): lax.ppermute(wave, AXES, [(at(p, host(turn, p, w)), at(p, host(turn + 1,...  11.5 us
    pallas_call x9, Pallas kernels, run(): pl.pallas_call(kernel, out_shape=shapes, in_specs=[SCALAR] * len(scalars)...  9.4 us
    ppermute x1, starting transfers between devices, local(): shared = lax.ppermute(sent, AXES, both)  7.91 us
    ppermute x1, waiting for transfers between devices, local(): e_in = lax.ppermute(o_e, AXES, first + swaps)  6.82 us
    ppermute x3, starting transfers between devices, exchanged(): lax.ppermute(value, 'pole', [(p, p ^ distance) for p in range(poles)])  6.06 us
    pallas_call x2, Pallas kernels, prepare(): pl.pallas_call(lambda slot, live, weight, pivot, factor, *outs: prepare_k...  5.68 us
  transfers between devices with their start and end apart: 11, of which 6 were waited for; matrix products, arithmetic and copies ran while one was open for 0% of the time, Pallas kernels for 7%

profile of v1, /device:TPU:29, one launch (start us, length us, event | category | flops | bytes accessed | tf_op | source)
XLA Modules:
  0.0 97.4 jit_solution(10496501069642047771)
XLA Ops:
  0.7 1.6 %copy-done = f32[2,2,2,256,256]{4,3,2,1,0:T(8,128)S(1)} copy-done((f32[2,2,2,256,256]{4,3,2,1,0:T(8,128)S(1)}, f32[2,2,2,256,256]{4,3,2,1,0:T(8,128)}, u32[]{:S(2)}) %copy-start) | copy-done | bytes 2097176
  2.3 1.6 %copy-done.2 = f32[2,2,2,256,256]{4,3,2,1,0:T(8,128)S(1)} copy-done((f32[2,2,2,256,256]{4,3,2,1,0:T(8,128)S(1)}, f32[2,2,2,256,256]{4,3,2,1,0:T(8,128)}, u32[]{:S(2)}) %copy-start.2) | copy-done | bytes 2097176
  3.9 0.7 copy-done.3
  5.2 2.8 %shard_map.60 = (bf16[4,256,256]{2,1,0:T(8,128)(2,1)S(1)}, bf16[4,256,256]{2,1,0:T(8,128)(2,1)S(1)}, bf16[4,256,256]{2,1,0:T(8,128)(2,1)S(1)}, bf16[4,256,256]{2...) custom-call(s32[1]{0:T(128)} %bitcast.1.slot, ...), custom_call_target="tpu_custom_call" | custom-call | flops 1207959552 | bytes 6291456 | tf_op jit(solution)/shard_map/pallas_call | solution.py:240
  8.1 0.8 copy-done.9
  8.8 0.8 copy-done.11
  9.6 0.8 copy-done.13
  10.4 0.8 copy-done.16
  11.2 3.1 %collective-permute-start = (f32[2,256,256]{2,1,0:T(8,128)S(1)}, f32[2,256,256]{2,1,0:T(8,128)S(1)}, u32[]{:S(2)}, u32[]{:S(2)}) collective-permute-start(f32[2,256,256]{2,1,0:T(8,128)S(1)} %get-tuple-element.26), channel_id=1, source_target_pairs={{2,3},{3,2},{4,5},{5,4},{6,7},{7,6},{10,11},{11,10},{12,13},{13,12... | collective-permute-start | bytes 1572872 | tf_op jit(solution)/shard_map/ppermute | solution.py:286
  14.3 2.2 %collective-permute-start.1 = (f32[2,264,128]{2,1,0:T(8,128)S(1)}, f32[2,264,128]{2,1,0:T(8,128)S(1)}, u32[]{:S(2)}, u32[]{:S(2)}) collective-permute-start(f32[2,264,128]{2,1,0:T(8,128)S(1)} %get-tuple-element.27.e), channel_id=1, source_target_pairs={{0,1},{8,9},{16,17},{24,25},{2,3},{3,2},{4,5},{5,4},{6,7},{7,6},{1... | collective-permute-start | bytes 811016 | tf_op jit(solution)/shard_map/ppermute | solution.py:284
  16.6 2.8 %shard_map.59 = (bf16[4,256,256]{2,1,0:T(8,128)(2,1)S(1)}, bf16[4,256,256]{2,1,0:T(8,128)(2,1)S(1)}, bf16[4,256,256]{2,1,0:T(8,128)(2,1)S(1)}, bf16[4,256,256]{2...) custom-call(s32[1]{0:T(128)} %bitcast.3.slot, ...), custom_call_target="tpu_custom_call" | custom-call | flops 1207959552 | bytes 6291456 | tf_op jit(solution)/shard_map/pallas_call | solution.py:240
  19.4 0.8 copy-done.7
  20.2 0.8 copy-done.19
  21.0 0.8 copy-done.21
  21.8 0.8 copy-done.23
  22.6 0.8 copy-done.26
  23.4 0.8 copy-done.29
  24.2 0.7 collective-permute-start.3
  24.9 6.8 %collective-permute-done.1.e_in.refs_0_ = f32[2,264,128]{2,1,0:T(8,128)S(1)} collective-permute-done((f32[2,264,128]{2,1,0:T(8,128)S(1)}, f32[2,264,128]{2,1,0:T(8,128)S(1)}, u32[]{:S(2)}, u32[]{:S(2)}) %collective-permute-start.1) | collective-permute-done | bytes 270368 | tf_op jit(solution)/shard_map/ppermute | solution.py:284
  31.7 1.0 %copy-done.24 = bf16[4,256,256]{2,1,0:T(8,128)(2,1)S(1)} copy-done((bf16[4,256,256]{2,1,0:T(8,128)(2,1)S(1)}, bf16[4,256,256]{2,1,0:T(8,128)(2,1)}, u32[]{:S(2)}) %copy-start.24) | copy-done | bytes 524312
  32.7 1.0 %copy-done.27 = bf16[4,256,256]{2,1,0:T(8,128)(2,1)S(1)} copy-done((bf16[4,256,256]{2,1,0:T(8,128)(2,1)S(1)}, bf16[4,256,256]{2,1,0:T(8,128)(2,1)}, u32[]{:S(2)}) %copy-start.27) | copy-done | bytes 524312
  33.8 0.7 collective-permute-start.2
  34.5 1.0 %copy-done.14 = bf16[4,256,256]{2,1,0:T(8,128)(2,1)S(1)} copy-done((bf16[4,256,256]{2,1,0:T(8,128)(2,1)S(1)}, bf16[4,256,256]{2,1,0:T(8,128)(2,1)}, u32[]{:S(2)}) %copy-start.14) | copy-done | bytes 524312
  35.5 1.0 %copy-done.17 = bf16[4,256,256]{2,1,0:T(8,128)(2,1)S(1)} copy-done((bf16[4,256,256]{2,1,0:T(8,128)(2,1)S(1)}, bf16[4,256,256]{2,1,0:T(8,128)(2,1)}, u32[]{:S(2)}) %copy-start.17) | copy-done | bytes 524312
  37.3 1.0 %copy-done.30 = f32[2,256,256]{2,1,0:T(8,128)S(1)} copy-done((f32[2,256,256]{2,1,0:T(8,128)S(1)}, f32[2,256,256]{2,1,0:T(8,128)}, u32[]{:S(2)}) %copy-start.30) | copy-done | bytes 524312
  38.3 1.6 %shard_map.61 = (bf16[4,256,256]{2,1,0:T(8,128)(2,1)S(1)}, bf16[4,256,256]{2,1,0:T(8,128)(2,1)S(1)}, f32[2,264,128]{2,1,0:T(8,128)S(1)}, bf16[4,256,256]{2,1,0:T...) custom-call(s32[1]{0:T(128)} %bitcast.2.odd, f32[2,256,256]{2,1,0:T(8,128)S(1)} %copy-done.30, ...), custom_call_target="tpu_custom_call" | custom-call | flops 1207959552 | bytes 1589248 | tf_op jit(solution)/shard_map/pallas_call | solution.py:214
  39.9 0.8 copy-done.31
  40.7 0.8 copy-done.33
  41.5 0.8 copy-done.37
  42.4 0.8 copy-done.35
  43.3 0.8 collective-permute-start.5
  44.1 1.0 %copy-done.36 = bf16[4,256,256]{2,1,0:T(8,128)(2,1)S(1)} copy-done((bf16[4,256,256]{2,1,0:T(8,128)(2,1)S(1)}, bf16[4,256,256]{2,1,0:T(8,128)(2,1)}, u32[]{:S(2)}) %copy-start.36) | copy-done | bytes 524312
  45.1 1.0 %copy-done.38 = bf16[4,256,256]{2,1,0:T(8,128)(2,1)S(1)} copy-done((bf16[4,256,256]{2,1,0:T(8,128)(2,1)S(1)}, bf16[4,256,256]{2,1,0:T(8,128)(2,1)}, u32[]{:S(2)}) %copy-start.38) | copy-done | bytes 524312
  46.2 1.0 copy-done.40
  47.1 1.6 %collective-permute-start.6 = (f32[2,264,128]{2,1,0:T(8,128)S(1)}, f32[2,264,128]{2,1,0:T(8,128)S(1)}, u32[]{:S(2)}, u32[]{:S(2)}) collective-permute-start(f32[2,264,128]{2,1,0:T(8,128)S(1)} %shard_map.65), channel_id=1, source_target_pairs={{5,7},{4,6},{12,14},{13,15},{21,23},{20,22},{28,30},{29,31}} | collective-permute-start | bytes 811016 | tf_op jit(solution)/shard_map/ppermute | solution.py:312
  48.8 11.5 %collective-permute-done.6.refs_3_ = f32[2,264,128]{2,1,0:T(8,128)S(1)} collective-permute-done((f32[2,264,128]{2,1,0:T(8,128)S(1)}, f32[2,264,128]{2,1,0:T(8,128)S(1)}, u32[]{:S(2)}, u32[]{:S(2)}) %collective-permute-start.6) | collective-permute-done | bytes 270368 | tf_op jit(solution)/shard_map/ppermute | solution.py:312
  60.3 1.0 %copy-done.34 = bf16[4,256,256]{2,1,0:T(8,128)(2,1)S(1)} copy-done((bf16[4,256,256]{2,1,0:T(8,128)(2,1)S(1)}, bf16[4,256,256]{2,1,0:T(8,128)(2,1)}, u32[]{:S(2)}) %copy-start.34) | copy-done | bytes 524312
  61.3 1.2 %shard_map.66 = (f32[2,264,128]{2,1,0:T(8,128)S(1)}, f32[2,264,128]{2,1,0:T(8,128)S(1)}) custom-call(s32[1]{0:T(128)} %bitcast.2.odd, bf16[4,256,256]{2,1,0:T(8,128)(2,1)S(1)} %copy-done.32, bf16[4,256,256]{2,1,0:T(8,128)(2,1)S(1)} %copy-done.34, f32[2,264,128]{2,1,0:T(8,128)S(1)} %get-tuple-element.30.ea, ...), custom_call_target="tpu_custom_call" | custom-call | flops 805306368 | bytes 2400256 | tf_op jit(solution)/shard_map/pallas_call | solution.py:214
  62.5 7.9 %collective-permute-start.7 = (f32[2,264,128]{2,1,0:T(8,128)S(1)}, f32[2,264,128]{2,1,0:T(8,128)S(1)}, u32[]{:S(2)}, u32[]{:S(2)}) collective-permute-start(f32[2,264,128]{2,1,0:T(8,128)S(1)} %get-tuple-element.38), channel_id=1, source_target_pairs={{0,1},{1,0},{2,3},{3,2},{4,5},{5,4},{6,7},{7,6},{8,9},{9,8},{10,11... | collective-permute-start | bytes 811016 | tf_op jit(solution)/shard_map/ppermute | solution.py:334
  70.5 2.7 %shard_map.67.refs_0_ = f32[2,776,128]{2,1,0:T(8,128)S(1)} custom-call(s32[1]{0:T(128)} %bitcast.3.slot, s32[1]{0:T(128)} %bitcast.core, f32[2,2]{1,0:T(2,128)S(1)} %copy-done.4, f32[2,264,128]{2,1,0:T(8,128)S(1)} %get-tuple-element.42.x, bf16[4,256,256]{2,1,0:T(8,128)(2,1)S(1)} %copy-done.20, bf16[4,256,256]{2,1,0:T(8,128)(2,1)S(1)} %copy-done.22, ...), custom_call_target="tpu_custom_call" | custom-call | flops 1409286144 | bytes 2908160 | tf_op jit(solution)/shard_map/pallas_call | solution.py:214
  73.2 1.2 %collective-permute-done.7.x = f32[2,264,128]{2,1,0:T(8,128)S(1)} collective-permute-done((f32[2,264,128]{2,1,0:T(8,128)S(1)}, f32[2,264,128]{2,1,0:T(8,128)S(1)}, u32[]{:S(2)}, u32[]{:S(2)}) %collective-permute-start.7) | collective-permute-done | bytes 270368 | tf_op jit(solution)/shard_map/ppermute | solution.py:334
  74.5 2.8 %shard_map.68 = f32[2,776,128]{2,1,0:T(8,128)S(1)} custom-call(s32[1]{0:T(128)} %bitcast.1.slot, s32[1]{0:T(128)} %bitcast.core, f32[2,2]{1,0:T(2,128)S(1)} %copy-done.4, f32[2,264,128]{2,1,0:T(8,128)S(1)} %collective-permute-done.7.x, bf16[4,256,256]{2,1,0:T(8,128)(2,1)S(1)} %copy-done.10, bf16[4,256,256]{2,1,0:T(8,128)(2,1)S(1)} %copy-done.12, ...), custom_call_target="tpu_custom_call" | custom-call | flops 1409286144 | bytes 3702784 | tf_op jit(solution)/shard_map/pallas_call | solution.py:214
  77.3 4.5 %collective-permute-start.8 = (f32[776,128]{1,0:T(8,128)S(1)}, f32[776,128]{1,0:T(8,128)S(1)}, u32[]{:S(2)}, u32[]{:S(2)}) collective-permute-start(f32[776,128]{1,0:T(8,128)S(1)} %slice_bitcast_fusion), channel_id=1, source_target_pairs={{0,8},{8,0},{16,24},{24,16},{1,9},{9,1},{17,25},{25,17},{2,10},{10... | collective-permute-start | bytes 1191944 | tf_op jit(solution)/shard_map/ppermute | solution.py:348
  81.8 1.4 %collective-permute-done.8 = f32[776,128]{1,0:T(8,128)S(1)} collective-permute-done((f32[776,128]{1,0:T(8,128)S(1)}, f32[776,128]{1,0:T(8,128)S(1)}, u32[]{:S(2)}, u32[]{:S(2)}) %collective-permute-start.8) | collective-permute-done | bytes 397344 | tf_op jit(solution)/shard_map/ppermute | solution.py:348
  83.5 10.2 %collective-permute-done.9 = f32[776,128]{1,0:T(8,128)S(1)} collective-permute-done((f32[776,128]{1,0:T(8,128)S(1)}, f32[776,128]{1,0:T(8,128)S(1)}, u32[]{:S(2)}, u32[]{:S(2)}) %collective-permute-start.9) | collective-permute-done | bytes 397344 | tf_op jit(solution)/shard_map/ppermute | solution.py:348
  93.7 1.3 %collective-permute-start.10 = (f32[776,128]{1,0:T(8,128)S(1)}, f32[776,128]{1,0:T(8,128)S(1)}, u32[]{:S(2)}, u32[]{:S(2)}) collective-permute-start(f32[776,128]{1,0:T(8,128)S(1)} %add.17.mine), channel_id=1, source_target_pairs={{0,8},{8,0},{16,24},{24,16},{1,9},{9,1},{17,25},{25,17},{2,10},{10... | collective-permute-start | bytes 1191944 | tf_op jit(solution)/shard_map/ppermute | solution.py:348
  95.0 1.4 %collective-permute-done.10.theirs = f32[776,128]{1,0:T(8,128)S(1)} collective-permute-done((f32[776,128]{1,0:T(8,128)S(1)}, f32[776,128]{1,0:T(8,128)S(1)}, u32[]{:S(2)}, u32[]{:S(2)}) %collective-permute-start.10) | collective-permute-done | bytes 397344 | tf_op jit(solution)/shard_map/ppermute | solution.py:348
  96.4 1.1 %shard_map.69 = (f32[2,256,256]{2,1,0:T(8,128)}, f32[2,256,256]{2,1,0:T(8,128)}) custom-call(s32[1]{0:T(128)} %bitcast.core, f32[776,128]{1,0:T(8,128)S(1)} %add.17.mine, f32[776,128]{1,0:T(8,128)S(1)} %collective-permute-done.10.theirs), custom_call_target="tpu_custom_call" | custom-call | bytes 794624 | tf_op jit(solution)/shard_map/pallas_call | solution.py:214
  (70 shorter events, 2.0 us)
Async XLA Ops:
  0.7 1.6 %copy-start = (f32[2,2,2,256,256]{4,3,2,1,0:T(8,128)S(1)}, f32[2,2,2,256,256]{4,3,2,1,0:T(8,128)}, u32[]{:S(2)}) copy-start(f32[2,2,2,256,256]{4,3,2,1,0:T(8,128)} %pivot.3) | copy-start | bytes 6291460
  2.3 1.6 %copy-start.2 = (f32[2,2,2,256,256]{4,3,2,1,0:T(8,128)S(1)}, f32[2,2,2,256,256]{4,3,2,1,0:T(8,128)}, u32[]{:S(2)}) copy-start(f32[2,2,2,256,256]{4,3,2,1,0:T(8,128)} %factor.3) | copy-start | bytes 6291460
  5.2 11.3 %copy-start.1 = (f32[2,2,2,256,256]{4,3,2,1,0:T(8,128)S(1)}, f32[2,2,2,256,256]{4,3,2,1,0:T(8,128)}, u32[]{:S(2)}) copy-start(f32[2,2,2,256,256]{4,3,2,1,0:T(8,128)} %pivot.3) | copy-start | bytes 6291460
  5.2 11.3 %copy-start.4 = (f32[2,2]{1,0:T(2,128)S(1)}, f32[2,2]{1,0:T(2,128)}, u32[]{:S(2)}) copy-start(f32[2,2]{1,0:T(2,128)} %weight.7) | copy-start | bytes 52
  5.2 11.3 %copy-start.6 = (s32[2]{0:T(128)S(1)}, s32[2]{0:T(128)}, u32[]{:S(2)}) copy-start(s32[2]{0:T(128)} %live.3) | copy-start | bytes 28
  8.0 0.8 copy-start.9
  8.8 0.8 copy-start.11
  10.4 0.8 copy-start.16
  11.2 26.0 %collective-permute-start = (f32[2,256,256]{2,1,0:T(8,128)S(1)}, f32[2,256,256]{2,1,0:T(8,128)S(1)}, u32[]{:S(2)}, u32[]{:S(2)}) collective-permute-start(f32[2,256,256]{2,1,0:T(8,128)S(1)} %get-tuple-element.26), channel_id=1, source_target_pairs={{2,3},{3,2},{4,5},{5,4},{6,7},{7,6},{10,11},{11,10},{12,13},{13,12... | collective-permute-start | bytes 1572872 | tf_op jit(solution)/shard_map/ppermute | solution.py:286
  14.3 17.4 %collective-permute-start.1 = (f32[2,264,128]{2,1,0:T(8,128)S(1)}, f32[2,264,128]{2,1,0:T(8,128)S(1)}, u32[]{:S(2)}, u32[]{:S(2)}) collective-permute-start(f32[2,264,128]{2,1,0:T(8,128)S(1)} %get-tuple-element.27.e), channel_id=1, source_target_pairs={{0,1},{8,9},{16,17},{24,25},{2,3},{3,2},{4,5},{5,4},{6,7},{7,6},{1... | collective-permute-start | bytes 811016 | tf_op jit(solution)/shard_map/ppermute | solution.py:284
  19.4 0.8 copy-start.7
  20.2 0.8 copy-start.19
  21.0 0.8 copy-start.21
  21.8 0.8 copy-start.23
  23.4 0.8 copy-start.29
  24.2 10.3 %collective-permute-start.3 = (f32[2,264,128]{2,1,0:T(8,128)S(1)}, f32[2,264,128]{2,1,0:T(8,128)S(1)}, u32[]{:S(2)}, u32[]{:S(2)}) collective-permute-start(f32[2,264,128]{2,1,0:T(8,128)S(1)} %get-tuple-element.25.e), channel_id=1, source_target_pairs={{0,1},{8,9},{16,17},{24,25}} | collective-permute-start | bytes 811016 | tf_op jit(solution)/shard_map/ppermute | solution.py:287
  31.7 1.0 %copy-start.24 = (bf16[4,256,256]{2,1,0:T(8,128)(2,1)S(1)}, bf16[4,256,256]{2,1,0:T(8,128)(2,1)}, u32[]{:S(2)}) copy-start(bf16[4,256,256]{2,1,0:T(8,128)(2,1)} %copy-done.23) | copy-start | bytes 1572868
  32.7 1.0 %copy-start.27 = (bf16[4,256,256]{2,1,0:T(8,128)(2,1)S(1)}, bf16[4,256,256]{2,1,0:T(8,128)(2,1)}, u32[]{:S(2)}) copy-start(bf16[4,256,256]{2,1,0:T(8,128)(2,1)} %copy-done.26) | copy-start | bytes 1572868
  33.8 7.7 %collective-permute-start.2 = (f32[2,264,128]{2,1,0:T(8,128)S(1)}, f32[2,264,128]{2,1,0:T(8,128)S(1)}, u32[]{:S(2)}, u32[]{:S(2)}) collective-permute-start(f32[2,264,128]{2,1,0:T(8,128)S(1)} %shard_map.62), channel_id=1, source_target_pairs={{1,3},{9,10},{17,19},{25,26}} | collective-permute-start | bytes 811016 | tf_op jit(solution)/shard_map/ppermute | solution.py:296
  34.5 1.0 %copy-start.14 = (bf16[4,256,256]{2,1,0:T(8,128)(2,1)S(1)}, bf16[4,256,256]{2,1,0:T(8,128)(2,1)}, u32[]{:S(2)}) copy-start(bf16[4,256,256]{2,1,0:T(8,128)(2,1)} %copy-done.13) | copy-start | bytes 1572868
  35.5 1.0 %copy-start.17 = (bf16[4,256,256]{2,1,0:T(8,128)(2,1)S(1)}, bf16[4,256,256]{2,1,0:T(8,128)(2,1)}, u32[]{:S(2)}) copy-start(bf16[4,256,256]{2,1,0:T(8,128)(2,1)} %copy-done.16) | copy-start | bytes 1572868
  36.6 5.0 %collective-permute-start.4 = (f32[2,264,128]{2,1,0:T(8,128)S(1)}, f32[2,264,128]{2,1,0:T(8,128)S(1)}, u32[]{:S(2)}, u32[]{:S(2)}) collective-permute-start(f32[2,264,128]{2,1,0:T(8,128)S(1)} %shard_map.63), channel_id=1, source_target_pairs={{1,2},{9,11},{17,18},{25,27}} | collective-permute-start | bytes 811016 | tf_op jit(solution)/shard_map/ppermute | solution.py:299
  37.2 1.0 %copy-start.30 = (f32[2,256,256]{2,1,0:T(8,128)S(1)}, f32[2,256,256]{2,1,0:T(8,128)}, u32[]{:S(2)}) copy-start(f32[2,256,256]{2,1,0:T(8,128)} %copy-done.29) | copy-start | bytes 1572868
  39.9 0.8 copy-start.31
  40.7 0.8 copy-start.33
  41.5 0.8 copy-start.37
  41.5 0.9 copy-start.39
  42.4 0.8 copy-start.35
  43.3 17.0 %copy-start.32 = (bf16[4,256,256]{2,1,0:T(8,128)(2,1)S(1)}, bf16[4,256,256]{2,1,0:T(8,128)(2,1)}, u32[]{:S(2)}) copy-start(bf16[4,256,256]{2,1,0:T(8,128)(2,1)} %copy-done.31) | copy-start | bytes 1572868
  43.3 0.8 collective-permute-start.5
  44.1 1.0 %copy-start.36 = (bf16[4,256,256]{2,1,0:T(8,128)(2,1)S(1)}, bf16[4,256,256]{2,1,0:T(8,128)(2,1)}, u32[]{:S(2)}) copy-start(bf16[4,256,256]{2,1,0:T(8,128)(2,1)} %copy-done.35) | copy-start | bytes 1572868
  45.1 1.0 %copy-start.38 = (bf16[4,256,256]{2,1,0:T(8,128)(2,1)S(1)}, bf16[4,256,256]{2,1,0:T(8,128)(2,1)}, u32[]{:S(2)}) copy-start(bf16[4,256,256]{2,1,0:T(8,128)(2,1)} %copy-done.37) | copy-start | bytes 1572868
  46.2 1.0 copy-start.40
  47.1 23.3 %copy-start.8 = (f32[4,264,128]{2,1,0:T(8,128)S(1)}, f32[4,264,128]{2,1,0:T(8,128)}, u32[]{:S(2)}) copy-start(f32[4,264,128]{2,1,0:T(8,128)} %copy-done.7) | copy-start | bytes 1622020
  47.1 23.3 %copy-start.20 = (bf16[4,256,256]{2,1,0:T(8,128)(2,1)S(1)}, bf16[4,256,256]{2,1,0:T(8,128)(2,1)}, u32[]{:S(2)}) copy-start(bf16[4,256,256]{2,1,0:T(8,128)(2,1)} %copy-done.19) | copy-start | bytes 1572868
  47.1 23.3 %copy-start.22 = (bf16[4,256,256]{2,1,0:T(8,128)(2,1)S(1)}, bf16[4,256,256]{2,1,0:T(8,128)(2,1)}, u32[]{:S(2)}) copy-start(bf16[4,256,256]{2,1,0:T(8,128)(2,1)} %copy-done.21) | copy-start | bytes 1572868
  47.1 23.3 %copy-start.25 = (bf16[4,256,256]{2,1,0:T(8,128)(2,1)S(1)}, bf16[4,256,256]{2,1,0:T(8,128)(2,1)}, u32[]{:S(2)}) copy-start(bf16[4,256,256]{2,1,0:T(8,128)(2,1)} %copy-done.23) | copy-start | bytes 1572868
  47.1 23.3 %copy-start.28 = (bf16[4,256,256]{2,1,0:T(8,128)(2,1)S(1)}, bf16[4,256,256]{2,1,0:T(8,128)(2,1)}, u32[]{:S(2)}) copy-start(bf16[4,256,256]{2,1,0:T(8,128)(2,1)} %copy-done.26) | copy-start | bytes 1572868
  47.1 13.1 %collective-permute-start.6 = (f32[2,264,128]{2,1,0:T(8,128)S(1)}, f32[2,264,128]{2,1,0:T(8,128)S(1)}, u32[]{:S(2)}, u32[]{:S(2)}) collective-permute-start(f32[2,264,128]{2,1,0:T(8,128)S(1)} %shard_map.65), channel_id=1, source_target_pairs={{5,7},{4,6},{12,14},{13,15},{21,23},{20,22},{28,30},{29,31}} | collective-permute-start | bytes 811016 | tf_op jit(solution)/shard_map/ppermute | solution.py:312
  60.3 1.0 %copy-start.34 = (bf16[4,256,256]{2,1,0:T(8,128)(2,1)S(1)}, bf16[4,256,256]{2,1,0:T(8,128)(2,1)}, u32[]{:S(2)}) copy-start(bf16[4,256,256]{2,1,0:T(8,128)(2,1)} %copy-done.33) | copy-start | bytes 1572868
  62.5 11.9 %collective-permute-start.7 = (f32[2,264,128]{2,1,0:T(8,128)S(1)}, f32[2,264,128]{2,1,0:T(8,128)S(1)}, u32[]{:S(2)}, u32[]{:S(2)}) collective-permute-start(f32[2,264,128]{2,1,0:T(8,128)S(1)} %get-tuple-element.38), channel_id=1, source_target_pairs={{0,1},{1,0},{2,3},{3,2},{4,5},{5,4},{6,7},{7,6},{8,9},{9,8},{10,11... | collective-permute-start | bytes 811016 | tf_op jit(solution)/shard_map/ppermute | solution.py:334
  70.5 4.0 %copy-start.10 = (bf16[4,256,256]{2,1,0:T(8,128)(2,1)S(1)}, bf16[4,256,256]{2,1,0:T(8,128)(2,1)}, u32[]{:S(2)}) copy-start(bf16[4,256,256]{2,1,0:T(8,128)(2,1)} %copy-done.9) | copy-start | bytes 1572868
  70.5 4.0 %copy-start.12 = (bf16[4,256,256]{2,1,0:T(8,128)(2,1)S(1)}, bf16[4,256,256]{2,1,0:T(8,128)(2,1)}, u32[]{:S(2)}) copy-start(bf16[4,256,256]{2,1,0:T(8,128)(2,1)} %copy-done.11) | copy-start | bytes 1572868
  70.5 4.0 %copy-start.15 = (bf16[4,256,256]{2,1,0:T(8,128)(2,1)S(1)}, bf16[4,256,256]{2,1,0:T(8,128)(2,1)}, u32[]{:S(2)}) copy-start(bf16[4,256,256]{2,1,0:T(8,128)(2,1)} %copy-done.13) | copy-start | bytes 1572868
  70.5 4.0 %copy-start.18 = (bf16[4,256,256]{2,1,0:T(8,128)(2,1)S(1)}, bf16[4,256,256]{2,1,0:T(8,128)(2,1)}, u32[]{:S(2)}) copy-start(bf16[4,256,256]{2,1,0:T(8,128)(2,1)} %copy-done.16) | copy-start | bytes 1572868
  77.3 5.9 %collective-permute-start.8 = (f32[776,128]{1,0:T(8,128)S(1)}, f32[776,128]{1,0:T(8,128)S(1)}, u32[]{:S(2)}, u32[]{:S(2)}) collective-permute-start(f32[776,128]{1,0:T(8,128)S(1)} %slice_bitcast_fusion), channel_id=1, source_target_pairs={{0,8},{8,0},{16,24},{24,16},{1,9},{9,1},{17,25},{25,17},{2,10},{10... | collective-permute-start | bytes 1191944 | tf_op jit(solution)/shard_map/ppermute | solution.py:348
  83.2 10.5 %collective-permute-start.9 = (f32[776,128]{1,0:T(8,128)S(1)}, f32[776,128]{1,0:T(8,128)S(1)}, u32[]{:S(2)}, u32[]{:S(2)}) collective-permute-start(f32[776,128]{1,0:T(8,128)S(1)} %fusion), channel_id=1, source_target_pairs={{0,16},{8,24},{16,0},{24,8},{1,17},{9,25},{17,1},{25,9},{2,18},{10... | collective-permute-start | bytes 1191944 | tf_op jit(solution)/shard_map/ppermute | solution.py:348
  93.7 2.6 %collective-permute-start.10 = (f32[776,128]{1,0:T(8,128)S(1)}, f32[776,128]{1,0:T(8,128)S(1)}, u32[]{:S(2)}, u32[]{:S(2)}) collective-permute-start(f32[776,128]{1,0:T(8,128)S(1)} %add.17.mine), channel_id=1, source_target_pairs={{0,8},{8,0},{16,24},{24,16},{1,9},{9,1},{17,25},{25,17},{2,10},{10... | collective-permute-start | bytes 1191944 | tf_op jit(solution)/shard_map/ppermute | solution.py:348
  (4 other events, 2.9 us)
